TPU v7x, 32 devices: a whole 2x2x4 slice. The times are simulated.
32 devices in a mesh: seq: 4 (over y, x), section: 4 (over z), mp: 2 (over core).
Axes of the slice: x: 2, y: 2, z: 4, core: 2. Of those that a mesh axis runs over, the one named last changes fastest.
Arguments:
- enc_rows: bfloat16 [4, 1024, 512], P('section', 'seq'), may hold values from -6 to 6
- proj_weight: bfloat16 [512, 8192], P(None, 'mp'), may hold values from -0.25 to 0.25
- row_owner: int32 [4, 1024], P('section', 'seq'), may hold values from -1 to 3, as said below
- grad_in: bfloat16 [4, 1024, 8192], P('section', 'seq', 'mp'), may hold values from -3 to 3
- adapter_gain: float32 [4, 8192], P('section', 'mp'), may hold values from 0.25 to 1.75
- adapter_down: bfloat16 [4, 64, 8192], P('section', None, 'mp'), may hold values from -0.375 to 0.375
- adapter_up: bfloat16 [4, 64, 8192], P('section', None, 'mp'), may hold values from -0.0625 to 0.0625
Outputs:
- soft_tokens: bfloat16 [4, 1024, 8192], P('section', 'seq', 'mp')
- enc_grad: float32 [4, 1024, 512], P('section', 'seq', 'mp')
Inputs may be any that keep to these rules, and one draw needn't show every extreme that they name: row_owner[s, r] is the reader device along seq of encoder row r of micro-batch s, or -1 for an empty row. Every reader receives 16 to 256 rows of a micro-batch, and one reader exactly 256. One encoder device holds at most 64 rows for one reader, and exactly 64 for that fullest reader.
All inputs are finite; a program needn't handle non-finite values.
Results may differ from a plain program's by a relative error of at most 0.0061.
Values may be sent and summed in bfloat16 or wider, within the bound.
A program may use at most 64 MiB of HBM per device.

v0:
```python
import jax
import jax.numpy as jnp
from jax import lax
from jax.sharding import PartitionSpec as P

TICKS = 2


def from_behind(value, axis, steps):
    count = lax.axis_size(axis)
    pairs = [(source, (source + steps) % count) for source in range(count)]
    return lax.ppermute(value, axis, pairs)


def pick_rows(values, row_index, keep_mask):
    picked = jnp.take(values, jnp.minimum(row_index, values.shape[0] - 1), axis=0)
    return jnp.where(keep_mask[:, None], picked, jnp.zeros_like(picked))


def adapter_back(carried, gain_row, down_rows, up_rows):
    partial_low = lax.dot_general(
        up_rows, carried, (((1,), (1,)), ((), ())), preferred_element_type=jnp.float32
    )
    reduced = lax.psum(partial_low, "mp").astype(jnp.bfloat16)
    spread = lax.dot_general(
        reduced, down_rows, (((0,), (0,)), ((), ())), preferred_element_type=jnp.float32
    )
    return (carried.astype(jnp.float32) + gain_row[None, :] * spread).astype(jnp.bfloat16)


def on_device(enc_rows, proj_weight, row_owner, grad_in, adapter_gain, adapter_down, adapter_up):
    readers = lax.axis_size("seq")
    owners = row_owner[0]
    slot_count = owners.shape[0]
    per_peer = slot_count // readers
    matches = (owners[:, None] == jnp.arange(readers, dtype=jnp.int32)[None, :]).astype(jnp.int32)
    before = jnp.cumsum(matches, axis=0) - matches
    order_rank = jnp.sum(matches * before, axis=1)
    live_in = owners >= 0
    target = jnp.where(live_in, owners * per_peer + order_rank, slot_count)
    source = (
        jnp.full((slot_count + 1,), slot_count, jnp.int32)
        .at[target]
        .set(jnp.arange(slot_count, dtype=jnp.int32))[:slot_count]
    )
    live_out = source < slot_count
    enc_block = enc_rows[0]
    projected = jnp.dot(enc_block, proj_weight, preferred_element_type=jnp.float32).astype(
        jnp.bfloat16
    )
    outgoing = pick_rows(projected, source, live_out)
    soft_block = lax.all_to_all(outgoing, "seq", split_axis=0, concat_axis=0, tiled=True)
    gain_row = adapter_gain[0]
    down_rows = adapter_down[0]
    up_rows = adapter_up[0]
    carried = grad_in[0]
    for tick_index in range(TICKS + 1):
        carried = adapter_back(carried, gain_row, down_rows, up_rows)
        if tick_index < TICKS:
            carried = from_behind(carried, "section", -1)
    returned = lax.all_to_all(carried, "seq", split_axis=0, concat_axis=0, tiled=True)
    own_grads = pick_rows(returned, target, live_in)
    partial_rows = lax.dot_general(
        own_grads, proj_weight, (((1,), (1,)), ((), ())), preferred_element_type=jnp.float32
    )
    row_grads = lax.psum_scatter(partial_rows, "mp", scatter_dimension=1, tiled=True)
    return (soft_block[None], row_grads[None])


def solution(mesh):
    placed = (
        P("section", "seq", None),
        P(None, "mp"),
        P("section", "seq"),
        P("section", "seq", "mp"),
        P("section", "mp"),
        P("section", None, "mp"),
        P("section", None, "mp"),
    )
    return jax.shard_map(
        on_device,
        mesh=mesh,
        in_specs=placed,
        out_specs=(P("section", "seq", "mp"), P("section", "seq", "mp")),
        check_vma=False,
    )
```

profile of v0, /device:TPU:0, one launch (start us, length us, event | category | flops | bytes accessed | tf_op | source)
XLA Modules:
  0.0 196.4 jit_solution(2431915075589629131)
XLA Ops:
  7.2 0.0 copy-start
  7.2 0.0 copy-start.1
  7.2 0.0 copy-start.3
  7.2 2.7 %fusion.2 = f32[64,256]{1,0:T(8,128)S(1)} fusion(bf16[1,256,4096]{2,1,0:T(8,128)(2,1)} %param.12, bf16[1,64,4096]{2,1,0:T(8,128)(2,1)} %param.15), kind=kOutput, calls=%fused_computation.11 | convolution fusion | flops 134217728 | bytes 2686976 | tf_op jit(solution)/shard_map/dot_general | solution.py:21
  9.9 3.9 %psum.21 = bf16[64,256]{1,0:T(8,128)(2,1)S(1)} all-reduce(f32[64,256]{1,0:T(8,128)S(1)} %fusion.2), channel_id=1, replica_groups=mesh['seq'=4,'section'=4,'mp'=2] {'mp'}, use_global_device_ids=true, to_apply=%region_4.6 | all-reduce | flops 16384 | bytes 98304 | tf_op jit(solution)/shard_map/psum | solution.py:24
  13.8 0.0 copy-done
  13.8 0.0 copy-done.1
  13.8 0.0 copy-done.3
  13.8 0.0 copy-start.2
  13.8 0.7 fusion.1
  14.5 4.8 %collective-permute-start = (bf16[256,4096]{1,0:T(8,128)(2,1)S(1)}, bf16[256,4096]{1,0:T(8,128)(2,1)S(1)}, u32[]{:S(2)}, u32[]{:S(2)}) collective-permute-start(bf16[256,4096]{1,0:T(8,128)(2,1)S(1)} %fusion.1), channel_id=1, source_target_pairs={{0,6},{2,0},{4,2},{6,4},{1,7},{3,1},{5,3},{7,5},{8,14},{10,8},{12,... | collective-permute-start | bytes 6291464 | tf_op jit(solution)/shard_map/ppermute | solution.py:12
  19.4 45.4 %collective-permute-done = bf16[256,4096]{1,0:T(8,128)(2,1)S(1)} collective-permute-done((bf16[256,4096]{1,0:T(8,128)(2,1)S(1)}, bf16[256,4096]{1,0:T(8,128)(2,1)S(1)}, u32[]{:S(2)}, u32[]{:S(2)}) %collective-permute-start) | collective-permute-done | bytes 2097184 | tf_op jit(solution)/shard_map/ppermute | solution.py:12
  64.8 0.0 copy-done.2
  64.8 0.7 convolution_bitcast_fusion.1
  65.5 3.8 %psum.22 = bf16[64,256]{0,1:T(8,128)(2,1)S(1)} all-reduce(f32[64,256]{0,1:T(8,128)S(1)} %convolution_bitcast_fusion.1), channel_id=1, replica_groups=mesh['seq'=4,'section'=4,'mp'=2] {'mp'}, use_global_device_ids=true, to_apply=%region_5.7 | all-reduce | flops 16384 | bytes 98304 | tf_op jit(solution)/shard_map/psum | solution.py:24
  69.3 0.0 copy-start.4
  69.3 2.0 %add_convert_fusion.1 = bf16[256,4096]{1,0:T(8,128)(2,1)} fusion(bf16[256,4096]{1,0:T(8,128)(2,1)S(1)} %collective-permute-done, f32[4096]{0:T(1024)S(1)} %bitcast.73, bf16[1,64,4096]{2,1,0:T(8,128)(2,1)S(1)} %copy-done, bf16[64,256]{0,1:T(8,128)(2,1)S(1)} %psum.22), kind=kOutput, calls=%fused_computation.10 | convolution fusion | flops 138412032 | bytes 4767744 | tf_op jit(solution)/shard_map/dot_general | solution.py:25
  71.4 4.3 %collective-permute-start.1 = (bf16[256,4096]{1,0:T(8,128)(2,1)}, bf16[256,4096]{1,0:T(8,128)(2,1)S(1)}, u32[]{:S(2)}, u32[]{:S(2)}) collective-permute-start(bf16[256,4096]{1,0:T(8,128)(2,1)} %add_convert_fusion.1), channel_id=1, source_target_pairs={{0,6},{2,0},{4,2},{6,4},{1,7},{3,1},{5,3},{7,5},{8,14},{10,8},{12,... | collective-permute-start | bytes 6291464 | tf_op jit(solution)/shard_map/ppermute | solution.py:12
  75.6 0.0 copy-done.4
  75.7 1.2 reduce-window.6
  76.9 0.1 slice.16
  76.9 0.1 copy.11
  77.1 0.1 copy.12
  77.2 0.1 add_bitcast_fusion
  77.3 1.4 scatter_custom_fusion
  78.7 4.9 %convolution_convert_fusion = bf16[256,4096]{1,0:T(8,128)(2,1)} fusion(bf16[512,4096]{1,0:T(8,128)(2,1)} %param.10, bf16[1,256,512]{2,1,0:T(8,128)(2,1)} %param.9), kind=kOutput, calls=%fused_computation.8 | convolution fusion | flops 1074790400 | bytes 6553600 | tf_op jit(solution)/shard_map/dot_general | solution.py:48
  83.6 37.8 %collective-permute-done.1 = bf16[256,4096]{1,0:T(8,128)(2,1)S(1)} collective-permute-done((bf16[256,4096]{1,0:T(8,128)(2,1)}, bf16[256,4096]{1,0:T(8,128)(2,1)S(1)}, u32[]{:S(2)}, u32[]{:S(2)}) %collective-permute-start.1) | collective-permute-done | bytes 2097184 | tf_op jit(solution)/shard_map/ppermute | solution.py:12
  121.4 0.7 convolution_bitcast_fusion
  122.1 3.8 %psum.23 = bf16[64,256]{0,1:T(8,128)(2,1)S(1)} all-reduce(f32[64,256]{0,1:T(8,128)S(1)} %convolution_bitcast_fusion), channel_id=1, replica_groups=mesh['seq'=4,'section'=4,'mp'=2] {'mp'}, use_global_device_ids=true, to_apply=%region_6.8 | all-reduce | flops 16384 | bytes 98304 | tf_op jit(solution)/shard_map/psum | solution.py:24
  125.9 2.0 %add_convert_fusion = bf16[256,4096]{1,0:T(8,128)(2,1)} fusion(bf16[256,4096]{1,0:T(8,128)(2,1)S(1)} %collective-permute-done.1, f32[4096]{0:T(1024)S(1)} %bitcast.74, bf16[1,64,4096]{2,1,0:T(8,128)(2,1)S(1)} %copy-done, bf16[64,256]{0,1:T(8,128)(2,1)S(1)} %psum.23), kind=kOutput, calls=%fused_computation.9 | convolution fusion | flops 138412032 | bytes 4767744 | tf_op jit(solution)/shard_map/dot_general | solution.py:25
  128.0 3.7 %all-to-all-start.1 = ((bf16[4,64,4096]{2,1,0:T(8,128)(2,1)}), bf16[4,64,4096]{2,1,0:T(8,128)(2,1)S(1)}, u32[]{:S(2)}, u32[]{:S(2)}) async-start(bf16[4,64,4096]{2,1,0:T(8,128)(2,1)} %bitcast.71), calls=%async_computation.1 | async-start | bytes 4194304 | tf_op jit(solution)/shard_map/all_to_all | solution.py:61
  131.7 7.0 %gather_fusion = bf16[256,4096]{1,0:T(8,128)(2,1)} fusion(bf16[256,4096]{1,0:T(8,128)(2,1)} %convolution_convert_fusion, s32[1024]{0:T(1024)S(1)} %pad_clamp_fusion.1), kind=kCustom, calls=%fused_computation.clone | custom fusion | bytes 4195328 | tf_op jit(solution)/shard_map/jit(_take)/gather | solution.py:16
  138.8 3.3 %select_select_fusion.2 = bf16[256,4096]{1,0:T(8,128)(2,1)} fusion(bf16[256,4096]{1,0:T(8,128)(2,1)} %gather_fusion, pred[256]{0:T(512)(128)(4,1)S(1)} %get-tuple-element.5, pred[256]{0:T(512)(128)(4,1)S(1)} %get-tuple-element.7), kind=kLoop, calls=%fused_computation.15 | loop fusion | flops 2097152 | bytes 4194816 | tf_op jit(solution)/shard_map/jit(_where)/select_n | solution.py:17
  142.0 15.2 %all-to-all-done.1 = bf16[4,64,4096]{2,1,0:T(8,128)(2,1)S(1)} async-done(((bf16[4,64,4096]{2,1,0:T(8,128)(2,1)}), bf16[4,64,4096]{2,1,0:T(8,128)(2,1)S(1)}, u32[]{:S(2)}, u32[]{:S(2)}) %all-to-all-start.1) | async-done | bytes 2097184 | tf_op jit(solution)/shard_map/all_to_all | solution.py:61
  157.2 4.4 %all-to-all-start = ((bf16[4,64,4096]{2,1,0:T(8,128)(2,1)}), bf16[4,64,4096]{2,1,0:T(8,128)(2,1)}, u32[]{:S(2)}, u32[]{:S(2)}) async-start(bf16[4,64,4096]{2,1,0:T(8,128)(2,1)} %bitcast.70), calls=%async_computation | async-start | bytes 4194304 | tf_op jit(solution)/shard_map/all_to_all | solution.py:52
  161.7 0.2 reduce-scatter.2.cloned.1.call-start
  161.9 3.1 %gather_fusion.1 = bf16[256,4096]{1,0:T(8,128)(2,1)} fusion(bf16[256,4096]{1,0:T(8,128)(2,1)S(1)} %bitcast.69, s32[1024]{0:T(1024)S(1)} %pad_clamp_fusion), kind=kCustom, calls=%fused_computation.1.clone | custom fusion | bytes 4195328 | tf_op jit(solution)/shard_map/jit(_take)/gather | solution.py:16
  165.0 4.9 %fusion.4 = f32[256,512]{1,0:T(8,128)} fusion(bf16[512,4096]{1,0:T(8,128)(2,1)} %param.10, bf16[256,4096]{1,0:T(8,128)(2,1)} %gather_fusion.1, pred[256]{0:T(512)(128)(4,1)S(1)} %get-tuple-element.3, pred[256]{0:T(512)(128)(4,1)S(1)} %get-tuple-element.8), kind=kOutput, calls=%fused_computation.14 | convolution fusion | flops 1075838976 | bytes 6816256 | tf_op jit(solution)/shard_map/dot_general | solution.py:63
  169.9 0.0 reduce-scatter.2.cloned.1.call-update
  170.0 16.5 %all-to-all-done = bf16[4,64,4096]{2,1,0:T(8,128)(2,1)} async-done(((bf16[4,64,4096]{2,1,0:T(8,128)(2,1)}), bf16[4,64,4096]{2,1,0:T(8,128)(2,1)}, u32[]{:S(2)}, u32[]{:S(2)}) %all-to-all-start) | async-done | bytes 2097184 | tf_op jit(solution)/shard_map/all_to_all | solution.py:52
  186.4 0.0 reduce-scatter.2.cloned.1.call-done
  186.4 3.1 %copy.16 = bf16[1,256,4096]{2,1,0:T(8,128)(2,1)} copy(bf16[1,256,4096]{2,1,0:T(8,128)(2,1)} %bitcast.10) | data formatting | bytes 4194304
  (10 shorter events, 0.1 us)
Async XLA Ops:
  7.2 6.6 %copy-start = (bf16[1,64,4096]{2,1,0:T(8,128)(2,1)S(1)}, bf16[1,64,4096]{2,1,0:T(8,128)(2,1)}, u32[]{:S(2)}) copy-start(bf16[1,64,4096]{2,1,0:T(8,128)(2,1)} %param.14) | copy-start | bytes 1572868
  7.2 6.6 %copy-start.1 = (bf16[1,256,4096]{2,1,0:T(8,128)(2,1)S(1)}, bf16[1,256,4096]{2,1,0:T(8,128)(2,1)}, u32[]{:S(2)}) copy-start(bf16[1,256,4096]{2,1,0:T(8,128)(2,1)} %param.12) | copy-start | bytes 6291460
  7.2 6.6 %copy-start.3 = (f32[1,4096]{1,0:T(1,128)S(1)}, f32[1,4096]{1,0:T(1,128)}, u32[]{:S(2)}) copy-start(f32[1,4096]{1,0:T(1,128)} %param.13) | copy-start | bytes 49156
  13.8 51.0 %copy-start.2 = (bf16[1,64,4096]{2,1,0:T(8,128)(2,1)S(1)}, bf16[1,64,4096]{2,1,0:T(8,128)(2,1)}, u32[]{:S(2)}) copy-start(bf16[1,64,4096]{2,1,0:T(8,128)(2,1)} %param.15) | copy-start | bytes 1572868
  14.5 50.2 %collective-permute-start = (bf16[256,4096]{1,0:T(8,128)(2,1)S(1)}, bf16[256,4096]{1,0:T(8,128)(2,1)S(1)}, u32[]{:S(2)}, u32[]{:S(2)}) collective-permute-start(bf16[256,4096]{1,0:T(8,128)(2,1)S(1)} %fusion.1), channel_id=1, source_target_pairs={{0,6},{2,0},{4,2},{6,4},{1,7},{3,1},{5,3},{7,5},{8,14},{10,8},{12,... | collective-permute-start | bytes 6291464 | tf_op jit(solution)/shard_map/ppermute | solution.py:12
  69.3 6.3 %copy-start.4 = (s32[1,256]{1,0:T(1,128)S(1)}, s32[1,256]{1,0:T(1,128)}, u32[]{:S(2)}) copy-start(s32[1,256]{1,0:T(1,128)} %param.11) | copy-start | bytes 3076
  71.4 50.0 %collective-permute-start.1 = (bf16[256,4096]{1,0:T(8,128)(2,1)}, bf16[256,4096]{1,0:T(8,128)(2,1)S(1)}, u32[]{:S(2)}, u32[]{:S(2)}) collective-permute-start(bf16[256,4096]{1,0:T(8,128)(2,1)} %add_convert_fusion.1), channel_id=1, source_target_pairs={{0,6},{2,0},{4,2},{6,4},{1,7},{3,1},{5,3},{7,5},{8,14},{10,8},{12,... | collective-permute-start | bytes 6291464 | tf_op jit(solution)/shard_map/ppermute | solution.py:12
  128.0 29.2 %all-to-all-start.1 = ((bf16[4,64,4096]{2,1,0:T(8,128)(2,1)}), bf16[4,64,4096]{2,1,0:T(8,128)(2,1)S(1)}, u32[]{:S(2)}, u32[]{:S(2)}) async-start(bf16[4,64,4096]{2,1,0:T(8,128)(2,1)} %bitcast.71), calls=%async_computation.1 | async-start | bytes 4194304 | tf_op jit(solution)/shard_map/all_to_all | solution.py:61
  157.2 29.2 %all-to-all-start = ((bf16[4,64,4096]{2,1,0:T(8,128)(2,1)}), bf16[4,64,4096]{2,1,0:T(8,128)(2,1)}, u32[]{:S(2)}, u32[]{:S(2)}) async-start(bf16[4,64,4096]{2,1,0:T(8,128)(2,1)} %bitcast.70), calls=%async_computation | async-start | bytes 4194304 | tf_op jit(solution)/shard_map/all_to_all | solution.py:52
  161.7 24.8 %reduce-scatter.2.cloned.1.call-start = ((), (), s32[]{:S(2)}) async-start(), calls=%async_computation.3 | async-start | bytes 786432 | tf_op jit(solution)/shard_map/reduce_scatter | solution.py:66
Sparse Core Ops, SparseCore 0:
  170.1 9.9 reduce-scatter.1
where the time goes:
time: 197 us; the launch traced here: 196 us
  waiting for transfers between devices  115 us (58%)
  matrix products  18.6 us (9%)
  starting transfers between devices  17.5 us (9%)
  local copies, waits for them, and re-layouts  15 us (8%)
  between operations  14.2 us (7%)
  blocking collectives  11.6 us (6%)
  other arithmetic  4.64 us (2%)
    ppermute x2, waiting for transfers between devices, from_behind(): return lax.ppermute(value, axis, pairs)  83.2 us
    all_to_all x1, waiting for transfers between devices, on_device(): lax.all_to_all(outgoing, 'seq', split_axis=0, concat_axis=0, tiled=True)  16.5 us
    all_to_all x1, waiting for transfers between devices, on_device(): lax.all_to_all(carried, 'seq', split_axis=0, concat_axis=0, tiled=True)  15.2 us
    psum x3, blocking collectives, adapter_back(): reduced = lax.psum(partial_low, 'mp').astype(jnp.bfloat16)  11.6 us
    gather x2, local copies, waits for them, and re-layouts, pick_rows(): jnp.take(values, jnp.minimum(row_index, values.shape[0] - 1), axis=0)  10.2 us
    ppermute x2, starting transfers between devices, from_behind(): return lax.ppermute(value, axis, pairs)  9.09 us
    dot_general x1, matrix products, on_device(): lax.dot_general(own_grads, proj_weight, (((1,), (1,)), ((), ())), preferr...  4.91 us
    dot_general x1, matrix products, on_device(): jnp.dot(enc_block, proj_weight, preferred_element_type=jnp.float32)  4.86 us
  transfers between devices with their start and end apart: 5, of which 4 were waited for; matrix products, arithmetic and copies ran while one was open for 13% of the time, Pallas kernels for 0%

commit v1 on v0

v1 whole, which is shorter than its diff:
```python
import functools

import jax
import jax.numpy as jnp
from jax import lax
from jax.experimental import pallas as pl
from jax.experimental.pallas import tpu as pltpu
from jax.sharding import PartitionSpec as P

TICKS = 2
MESH = pl.DeviceIdType.MESH
F32, BF16 = jnp.float32, jnp.bfloat16


def times(a, b):
    return jnp.dot(a, b, preferred_element_type=F32)


def times_t(a, b):
    return lax.dot_general(a, b, (((1,), (1,)), ((), ())), preferred_element_type=F32)


def aligned(value, unit):
    return pl.multiple_of(value, unit)


def kernel(
    counts,
    enc_hbm, proj_hbm, owner_hbm, grad_hbm, gain_hbm, down_hbm, up_hbm,
    soft_hbm, out_hbm,
    enc, owner, gain, down, x, w, staged, routed, pick_t, soft,
    part, part_in, low, low_in, late, late_in,
    home, home_in, tail, tail_in, q_own, q_in, m_own, m_in, mix, out,
    load_sem, store_sem, send_sem, recv_sem,
):
    n_q, n_z, n_m = counts
    q, z, m = lax.axis_index("seq"), lax.axis_index("section"), lax.axis_index("mp")
    slots, width = enc.shape
    rank, features = down.shape
    columns = width // n_m
    per = slots // n_q
    share = features // n_q

    def device(dq, dz, dm):
        return (lax.rem(q + dq % n_q, n_q), lax.rem(z + dz % n_z, n_z), lax.rem(m + dm % n_m, n_m))

    used = [0, 0, 0]
    sent = []

    def load(src, dst):
        copy = pltpu.make_async_copy(src, dst, load_sem.at[used[0]])
        used[0] += 1
        copy.start()
        return copy

    def store(src, dst):
        copy = pltpu.make_async_copy(src, dst, store_sem.at[used[1]])
        used[1] += 1
        copy.start()
        return copy

    def send(src, dst, offsets):
        copy = pltpu.make_async_remote_copy(
            src_ref=src, dst_ref=dst,
            send_sem=send_sem.at[used[2]], recv_sem=recv_sem.at[used[2]],
            device_id=device(*offsets), device_id_type=MESH,
        )
        used[2] += 1
        copy.start()
        sent.append(copy)
        return copy

    owner_load = load(owner_hbm, owner)
    enc_load = load(enc_hbm.at[0], enc)
    low_load = load(up_hbm.at[0], w.at[pl.ds(width, rank)])
    grad_load = load(grad_hbm.at[0], x.at[pl.ds(0, slots)])
    gain_load = load(gain_hbm, gain)
    down_load = load(down_hbm.at[0], down)
    proj_loads = [
        load(proj_hbm.at[pl.ds(j * columns, columns)], w.at[pl.ds(j * columns, columns)])
        for j in range(n_m)
    ]

    targets = {(dq, 0, 0) for dq in range(1, n_q)}
    targets |= {(0, dz % n_z, 0) for dz in (1, TICKS, -1)}
    targets |= {(dq, -TICKS % n_z, 0) for dq in range(n_q)}
    targets |= {(0, 0, dm) for dm in range(1, n_m)}
    barrier = pltpu.get_barrier_semaphore()
    for dq, dz, dm in sorted(targets):
        pl.semaphore_signal(barrier, inc=1, device_id=device(-dq, -dz, -dm), device_id_type=MESH)
    pl.semaphore_wait(barrier, len(targets))

    own_share = pl.ds(aligned(q * share, share), share)
    up_rows = [pl.ds(width + tick * rank, rank) for tick in range(TICKS + 1)]
    up_sends = [
        send(up_hbm.at[0, :, own_share], w.at[up_rows[tick], own_share], (0, tick, 0))
        for tick in range(1, TICKS + 1)
    ]

    owner_load.wait()
    owners = owner[...].astype(F32)
    readers = lax.broadcasted_iota(jnp.int32, (max(8, n_q), slots), 0).astype(F32)
    matches = jnp.where(owners == readers, 1.0, 0.0)
    row_at = lax.broadcasted_iota(jnp.int32, (slots, slots), 0)
    column_at = lax.broadcasted_iota(jnp.int32, (slots, slots), 1)
    earlier = jnp.where(row_at < column_at, 1.0, 0.0).astype(BF16)
    before = times(matches.astype(BF16), earlier)
    order_rank = jnp.sum(matches * before, axis=0, keepdims=True)
    target = jnp.where(owners >= 0.0, owners * per + order_rank, -1.0)
    pick = jnp.where(row_at.astype(F32) == target, 1.0, 0.0)
    enc_load.wait()
    staged[...] = times(pick.astype(BF16), enc[...]).astype(BF16)
    own_rows = pl.ds(aligned(q * per, per), per)

    def rows_of(dq):
        return pl.ds(aligned(lax.rem(q + dq, n_q) * per, per), per)

    enc_sends = [
        send(staged.at[rows_of(dq)], routed.at[own_rows], (dq, 0, 0)) for dq in range(1, n_q)
    ]
    routed[own_rows, :] = staged[own_rows, :]
    pick_t[...] = jnp.transpose(pick).astype(BF16)

    grad_load.wait()
    low_load.wait()
    low[...] = times_t(x[pl.ds(0, slots), :], w[up_rows[0], :])
    low_sends = [send(low, low_in.at[dm - 1], (0, 0, dm)) for dm in range(1, n_m)]
    down_load.wait()
    gain_load.wait()
    x[pl.ds(slots, rank), :] = (gain[...] * down[...].astype(F32)).astype(BF16)
    for j in range(n_m):
        proj_loads[j].wait()
        part[j] = times_t(x[...], w[pl.ds(j * columns, columns), :])
    part_sends = [
        send(part.at[lax.rem(m + dm, n_m)], part_in.at[dm - 1], (0, 0, dm)) for dm in range(1, n_m)
    ]

    up_spread = []
    for tick in range(1, TICKS + 1):
        up_sends[tick - 1].wait_recv()
        up_spread += [
            send(w.at[up_rows[tick], own_share], w.at[up_rows[tick], own_share], (dq, 0, 0))
            for dq in range(1, n_q)
        ]

    for copy in low_sends + part_sends:
        copy.wait_recv()
    u_own = low[...]
    sums = part[m]
    for dm in range(1, n_m):
        u_own += low_in[dm - 1]
        sums += part_in[dm - 1]
    u_own = u_own.astype(BF16)
    q_own[...] = sums[slots:]
    home[...] = (sums[:slots] + times(u_own, sums[slots:].astype(BF16))).astype(BF16)
    home_sends = [
        send(home.at[rows_of(dq)], home_in.at[own_rows], (dq, -TICKS, 0)) for dq in range(n_q)
    ]
    q_send = send(q_own, q_in, (0, -1, 0))

    for copy in enc_sends:
        copy.wait_recv()
    stores = []
    tile = min(512, features)
    for start in range(0, features, tile):
        at = pl.ds(start, tile)
        soft[:, at] = times(routed[...], w[pl.ds(0, width), at]).astype(BF16)
        stores.append(store(soft.at[:, at], soft_hbm.at[0, :, at]))

    for copy in up_spread:
        copy.wait_recv()
    late[...] = times_t(x[...], w[pl.ds(width + rank, TICKS * rank), :])
    late_sends = [send(late, late_in.at[dm - 1], (0, 0, dm)) for dm in range(1, n_m)]
    for copy in late_sends:
        copy.wait_recv()
    sums = late[...]
    for dm in range(1, n_m):
        sums += late_in[dm - 1]
    m_own[...] = sums[slots:]
    m_send = send(m_own, m_in, (0, -1, 0))
    tail[...] = (sums[:slots] + times(u_own, sums[slots:].astype(BF16))).astype(BF16)
    tail_sends = [
        send(tail.at[rows_of(dq)], tail_in.at[own_rows], (dq, -TICKS, 0)) for dq in range(n_q)
    ]

    for copy in home_sends:
        copy.wait_recv()
    out[...] = times(pick_t[...], home_in[...])
    q_send.wait_recv()
    m_send.wait_recv()
    mix[pl.ds(0, rank), :] = (
        q_in[...] + times(m_in[...][:, :rank].astype(BF16), q_own[...].astype(BF16))
    ).astype(BF16)
    mix[pl.ds(rank, rank), :] = q_own[...].astype(BF16)
    for copy in tail_sends:
        copy.wait_recv()
    out[...] += times(times(pick_t[...], tail_in[...]).astype(BF16), mix[...])
    stores.append(store(out, out_hbm.at[0]))
    for copy in sent:
        copy.wait_send()
    for copy in stores:
        copy.wait()


def on_device(enc_rows, proj_weight, row_owner, grad_in, adapter_gain, adapter_down, adapter_up):
    counts = tuple(lax.axis_size(axis) for axis in ("seq", "section", "mp"))
    n_q, n_z, n_m = counts
    _, slots, width = enc_rows.shape
    _, rank, features = adapter_down.shape
    columns = width // n_m
    tiles = features // min(512, features)
    messages = TICKS + (n_q - 1) * (1 + TICKS) + 3 * (n_m - 1) + 2 * n_q + 2
    flops = 2 * slots * features * (2 * width + 3 * rank)
    vmem = pltpu.VMEM
    return pl.pallas_call(
        functools.partial(kernel, counts),
        out_shape=(
            jax.ShapeDtypeStruct((1, slots, features), BF16),
            jax.ShapeDtypeStruct((1, slots, columns), F32),
        ),
        in_specs=[pl.BlockSpec(memory_space=pl.ANY)] * 7,
        out_specs=(pl.BlockSpec(memory_space=pl.ANY),) * 2,
        scratch_shapes=[
            vmem((slots, width), BF16),
            vmem((1, slots), jnp.int32),
            vmem((1, features), F32),
            vmem((rank, features), BF16),
            vmem((slots + rank, features), BF16),
            vmem((width + (TICKS + 1) * rank, features), BF16),
            vmem((slots, width), BF16),
            vmem((slots, width), BF16),
            vmem((slots, slots), BF16),
            vmem((slots, features), BF16),
            vmem((n_m, slots + rank, columns), F32),
            vmem((n_m - 1, slots + rank, columns), F32),
            vmem((slots, rank), F32),
            vmem((n_m - 1, slots, rank), F32),
            vmem((slots + rank, TICKS * rank), F32),
            vmem((n_m - 1, slots + rank, TICKS * rank), F32),
            vmem((slots, columns), BF16),
            vmem((slots, columns), BF16),
            vmem((slots, TICKS * rank), BF16),
            vmem((slots, TICKS * rank), BF16),
            vmem((rank, columns), F32),
            vmem((rank, columns), F32),
            vmem((rank, TICKS * rank), F32),
            vmem((rank, TICKS * rank), F32),
            vmem((TICKS * rank, columns), BF16),
            vmem((slots, columns), F32),
            pltpu.SemaphoreType.DMA((6 + n_m,)),
            pltpu.SemaphoreType.DMA((tiles + 1,)),
            pltpu.SemaphoreType.DMA((messages,)),
            pltpu.SemaphoreType.DMA((messages,)),
        ],
        compiler_params=pltpu.CompilerParams(
            collective_id=0, has_side_effects=True, vmem_limit_bytes=48 * 1024 * 1024
        ),
        cost_estimate=pl.CostEstimate(flops=flops, bytes_accessed=12 * 1024 * 1024, transcendentals=0),
    )(enc_rows, proj_weight, row_owner, grad_in, adapter_gain, adapter_down, adapter_up)


def solution(mesh):
    placed = (
        P("section", "seq", None),
        P(None, "mp"),
        P("section", "seq"),
        P("section", "seq", "mp"),
        P("section", "mp"),
        P("section", None, "mp"),
        P("section", None, "mp"),
    )
    return jax.shard_map(
        on_device,
        mesh=mesh,
        in_specs=placed,
        out_specs=(P("section", "seq", "mp"), P("section", "seq", "mp")),
        check_vma=False,
    )
```

time: 197 us -> 43.5 us (0.22)
  the two profiles are of different devices: /device:TPU:0 before, /device:TPU:9 now
where the time goes in v1:
time: 43.5 us; the launch traced here: 43.1 us
  Pallas kernels  34.4 us (79%)
  local copies, waits for them, and re-layouts  8.03 us (18%)
  between operations  0.65 us (1%)
    pallas_call x1, Pallas kernels, on_device(): pl.pallas_call(functools.partial(kernel, counts), out_shape=(jax.ShapeDty...  34.4 us
    unnamed x14, local copies, waits for them, and re-layouts  8.03 us

profile of v1, /device:TPU:9, one launch (start us, length us, event | category | flops | bytes accessed | tf_op | source)
XLA Modules:
  0.0 43.1 jit_solution(14461716485594122172)
XLA Ops:
  0.6 0.0 copy-start
  0.6 1.6 %copy-done = bf16[1,256,4096]{2,1,0:T(8,128)(2,1)S(1)} copy-done((bf16[1,256,4096]{2,1,0:T(8,128)(2,1)S(1)}, bf16[1,256,4096]{2,1,0:T(8,128)(2,1)}, u32[]{:S(2)}) %copy-start) | copy-done | bytes 2097176
  2.2 0.0 copy-start.1
  2.2 1.0 %copy-done.1 = bf16[1,64,4096]{2,1,0:T(8,128)(2,1)S(1)} copy-done((bf16[1,64,4096]{2,1,0:T(8,128)(2,1)S(1)}, bf16[1,64,4096]{2,1,0:T(8,128)(2,1)}, u32[]{:S(2)}) %copy-start.1) | copy-done | bytes 524312
  3.3 0.0 copy-start.2
  3.3 1.0 %copy-done.2 = bf16[1,64,4096]{2,1,0:T(8,128)(2,1)S(1)} copy-done((bf16[1,64,4096]{2,1,0:T(8,128)(2,1)S(1)}, bf16[1,64,4096]{2,1,0:T(8,128)(2,1)}, u32[]{:S(2)}) %copy-start.2) | copy-done | bytes 524312
  4.3 0.0 copy-start.3
  4.3 0.9 %copy-done.3 = bf16[1,256,512]{2,1,0:T(8,128)(2,1)S(1)} copy-done((bf16[1,256,512]{2,1,0:T(8,128)(2,1)S(1)}, bf16[1,256,512]{2,1,0:T(8,128)(2,1)}, u32[]{:S(2)}) %copy-start.3) | copy-done | bytes 262168
  5.3 0.0 copy-start.4
  5.3 0.7 %copy-done.4 = f32[1,4096]{1,0:T(1,128)S(1)} copy-done((f32[1,4096]{1,0:T(1,128)S(1)}, f32[1,4096]{1,0:T(1,128)}, u32[]{:S(2)}) %copy-start.4) | copy-done | bytes 16408
  6.0 0.0 copy-start.5
  6.0 0.7 %copy-done.5 = s32[1,256]{1,0:T(1,128)S(1)} copy-done((s32[1,256]{1,0:T(1,128)S(1)}, s32[1,256]{1,0:T(1,128)}, u32[]{:S(2)}) %copy-start.5) | copy-done | bytes 1048
  6.7 34.4 %shard_map.86 = (bf16[1,256,4096]{2,1,0:T(8,128)(2,1)S(1)}, f32[1,256,256]{2,1,0:T(8,128)S(1)}) custom-call(bf16[1,256,512]{2,1,0:T(8,128)(2,1)S(1)} %copy-done.3, bf16[512,4096]{1,0:T(8,128)(2,1)} %proj_hbm.1, s32[1,256]{1,0:T(1,128)S(1)} %copy-done.5, bf16[1,256,4096]{2,1,0:T(8,128)(2,1)S(1)} %copy-done, f32[1,4096]{1,0:T(1,128)S(1)} %copy-done.4, ...), custom_call_target="tpu_custom_call" | custom-call | flops 2550136832 | bytes 12582912 | tf_op jit(solution)/shard_map/pallas_call | solution.py:215
  41.1 1.3 %copy.11 = bf16[1,256,4096]{2,1,0:T(8,128)(2,1)} copy(bf16[1,256,4096]{2,1,0:T(8,128)(2,1)S(1)} %get-tuple-element.4) | data formatting | bytes 4194304
  42.4 0.7 %copy.12 = f32[1,256,256]{2,1,0:T(8,128)} copy(f32[1,256,256]{2,1,0:T(8,128)S(1)} %get-tuple-element.5) | data formatting | bytes 524288
Async XLA Ops:
  0.6 1.6 %copy-start = (bf16[1,256,4096]{2,1,0:T(8,128)(2,1)S(1)}, bf16[1,256,4096]{2,1,0:T(8,128)(2,1)}, u32[]{:S(2)}) copy-start(bf16[1,256,4096]{2,1,0:T(8,128)(2,1)} %grad_hbm.1) | copy-start | bytes 6291460
  2.2 1.0 %copy-start.1 = (bf16[1,64,4096]{2,1,0:T(8,128)(2,1)S(1)}, bf16[1,64,4096]{2,1,0:T(8,128)(2,1)}, u32[]{:S(2)}) copy-start(bf16[1,64,4096]{2,1,0:T(8,128)(2,1)} %down_hbm.1) | copy-start | bytes 1572868
  3.3 1.0 %copy-start.2 = (bf16[1,64,4096]{2,1,0:T(8,128)(2,1)S(1)}, bf16[1,64,4096]{2,1,0:T(8,128)(2,1)}, u32[]{:S(2)}) copy-start(bf16[1,64,4096]{2,1,0:T(8,128)(2,1)} %up_hbm.1) | copy-start | bytes 1572868
  4.3 0.9 %copy-start.3 = (bf16[1,256,512]{2,1,0:T(8,128)(2,1)S(1)}, bf16[1,256,512]{2,1,0:T(8,128)(2,1)}, u32[]{:S(2)}) copy-start(bf16[1,256,512]{2,1,0:T(8,128)(2,1)} %enc_hbm.1) | copy-start | bytes 786436
  5.3 0.7 %copy-start.4 = (f32[1,4096]{1,0:T(1,128)S(1)}, f32[1,4096]{1,0:T(1,128)}, u32[]{:S(2)}) copy-start(f32[1,4096]{1,0:T(1,128)} %gain_hbm.1) | copy-start | bytes 49156
  6.0 0.7 %copy-start.5 = (s32[1,256]{1,0:T(1,128)S(1)}, s32[1,256]{1,0:T(1,128)}, u32[]{:S(2)}) copy-start(s32[1,256]{1,0:T(1,128)} %owner_hbm.1) | copy-start | bytes 3076

commit v2 on v1

--- a/solution.py
+++ b/solution.py
@@ -25,12 +25,12 @@
 
 
 def kernel(
-    counts,
+    counts, pieces,
     enc_hbm, proj_hbm, owner_hbm, grad_hbm, gain_hbm, down_hbm, up_hbm,
     soft_hbm, out_hbm,
     enc, owner, gain, down, x, w, staged, routed, pick_t, soft,
     part, part_in, low, low_in, late, late_in,
-    home, home_in, tail, tail_in, q_own, q_in, m_own, m_in, mix, out,
+    home, home_in, tail, tail_in, q_own, q_in, m_own, m_in, out,
     load_sem, store_sem, send_sem, recv_sem,
 ):
     n_q, n_z, n_m = counts
@@ -82,20 +82,12 @@
     ]
 
     targets = {(dq, 0, 0) for dq in range(1, n_q)}
-    targets |= {(0, dz % n_z, 0) for dz in (1, TICKS, -1)}
+    targets |= {(0, 1, 0), (0, -1 % n_z, 0)}
     targets |= {(dq, -TICKS % n_z, 0) for dq in range(n_q)}
     targets |= {(0, 0, dm) for dm in range(1, n_m)}
     barrier = pltpu.get_barrier_semaphore()
     for dq, dz, dm in sorted(targets):
         pl.semaphore_signal(barrier, inc=1, device_id=device(-dq, -dz, -dm), device_id_type=MESH)
-    pl.semaphore_wait(barrier, len(targets))
-
-    own_share = pl.ds(aligned(q * share, share), share)
-    up_rows = [pl.ds(width + tick * rank, rank) for tick in range(TICKS + 1)]
-    up_sends = [
-        send(up_hbm.at[0, :, own_share], w.at[up_rows[tick], own_share], (0, tick, 0))
-        for tick in range(1, TICKS + 1)
-    ]
 
     owner_load.wait()
     owners = owner[...].astype(F32)
@@ -110,6 +102,29 @@
     pick = jnp.where(row_at.astype(F32) == target, 1.0, 0.0)
     enc_load.wait()
     staged[...] = times(pick.astype(BF16), enc[...]).astype(BF16)
+    pl.semaphore_wait(barrier, len(targets))
+
+    piece = share // pieces
+    up_rows = [pl.ds(width + tick * rank, rank) for tick in range(TICKS + 1)]
+
+    def piece_at(h):
+        return pl.ds(aligned(q * share + h * piece, 128), piece)
+
+    ring = [
+        [
+            send(up_hbm.at[0, :, piece_at(h)], w.at[up_rows[1], piece_at(h)], (0, 1, 0))
+            for h in range(pieces)
+        ]
+    ] + [[] for _ in range(1, TICKS)]
+    spread = [[] for _ in range(TICKS)]
+
+    def pass_on(tick, h):
+        ring[tick][h].wait_recv()
+        here = w.at[up_rows[tick + 1], piece_at(h)]
+        if tick + 1 < TICKS:
+            ring[tick + 1].append(send(here, w.at[up_rows[tick + 2], piece_at(h)], (0, 1, 0)))
+        spread[tick] += [send(here, here, (dq, 0, 0)) for dq in range(1, n_q)]
+
     own_rows = pl.ds(aligned(q * per, per), per)
 
     def rows_of(dq):
@@ -119,7 +134,6 @@
         send(staged.at[rows_of(dq)], routed.at[own_rows], (dq, 0, 0)) for dq in range(1, n_q)
     ]
     routed[own_rows, :] = staged[own_rows, :]
-    pick_t[...] = jnp.transpose(pick).astype(BF16)
 
     grad_load.wait()
     low_load.wait()
@@ -128,20 +142,16 @@
     down_load.wait()
     gain_load.wait()
     x[pl.ds(slots, rank), :] = (gain[...] * down[...].astype(F32)).astype(BF16)
+    pass_on(0, 0)
     for j in range(n_m):
         proj_loads[j].wait()
         part[j] = times_t(x[...], w[pl.ds(j * columns, columns), :])
     part_sends = [
         send(part.at[lax.rem(m + dm, n_m)], part_in.at[dm - 1], (0, 0, dm)) for dm in range(1, n_m)
     ]
-
-    up_spread = []
-    for tick in range(1, TICKS + 1):
-        up_sends[tick - 1].wait_recv()
-        up_spread += [
-            send(w.at[up_rows[tick], own_share], w.at[up_rows[tick], own_share], (dq, 0, 0))
-            for dq in range(1, n_q)
-        ]
+    for h in range(1, pieces):
+        pass_on(0, h)
+    pick_t[...] = jnp.transpose(pick).astype(BF16)
 
     for copy in low_sends + part_sends:
         copy.wait_recv()
@@ -153,6 +163,9 @@
     u_own = u_own.astype(BF16)
     q_own[...] = sums[slots:]
     home[...] = (sums[:slots] + times(u_own, sums[slots:].astype(BF16))).astype(BF16)
+    for tick in range(1, TICKS):
+        for h in range(pieces):
+            pass_on(tick, h)
     home_sends = [
         send(home.at[rows_of(dq)], home_in.at[own_rows], (dq, -TICKS, 0)) for dq in range(n_q)
     ]
@@ -167,34 +180,37 @@
         soft[:, at] = times(routed[...], w[pl.ds(0, width), at]).astype(BF16)
         stores.append(store(soft.at[:, at], soft_hbm.at[0, :, at]))
 
-    for copy in up_spread:
-        copy.wait_recv()
-    late[...] = times_t(x[...], w[pl.ds(width + rank, TICKS * rank), :])
-    late_sends = [send(late, late_in.at[dm - 1], (0, 0, dm)) for dm in range(1, n_m)]
-    for copy in late_sends:
-        copy.wait_recv()
-    sums = late[...]
-    for dm in range(1, n_m):
-        sums += late_in[dm - 1]
-    m_own[...] = sums[slots:]
+    def layer_products(tick):
+        for copy in spread[tick]:
+            copy.wait_recv()
+        late[tick] = times_t(x[...], w[up_rows[tick + 1], :])
+        late_sends = [send(late.at[tick], late_in.at[tick, dm - 1], (0, 0, dm)) for dm in range(1, n_m)]
+        for copy in late_sends:
+            copy.wait_recv()
+        sums = late[tick]
+        for dm in range(1, n_m):
+            sums += late_in[tick, dm - 1]
+        tail[tick] = (sums[:slots] + times(u_own, sums[slots:].astype(BF16))).astype(BF16)
+        tail_sends = [
+            send(tail.at[tick, rows_of(dq)], tail_in.at[tick, own_rows], (dq, -TICKS, 0))
+            for dq in range(n_q)
+        ]
+        return tail_sends, sums[slots:]
+
+    tail_sends, low_mix = layer_products(0)
+    m_own[...] = low_mix
     m_send = send(m_own, m_in, (0, -1, 0))
-    tail[...] = (sums[:slots] + times(u_own, sums[slots:].astype(BF16))).astype(BF16)
-    tail_sends = [
-        send(tail.at[rows_of(dq)], tail_in.at[own_rows], (dq, -TICKS, 0)) for dq in range(n_q)
-    ]
-
-    for copy in home_sends:
-        copy.wait_recv()
-    out[...] = times(pick_t[...], home_in[...])
-    q_send.wait_recv()
-    m_send.wait_recv()
-    mix[pl.ds(0, rank), :] = (
-        q_in[...] + times(m_in[...][:, :rank].astype(BF16), q_own[...].astype(BF16))
-    ).astype(BF16)
-    mix[pl.ds(rank, rank), :] = q_own[...].astype(BF16)
-    for copy in tail_sends:
-        copy.wait_recv()
-    out[...] += times(times(pick_t[...], tail_in[...]).astype(BF16), mix[...])
+    last_sends, _ = layer_products(1)
+
+    for copy in home_sends + [q_send, m_send] + tail_sends:
+        copy.wait_recv()
+    own_low = q_own[...].astype(BF16)
+    mix = (q_in[...] + times(m_in[...].astype(BF16), own_low)).astype(BF16)
+    behind = times(pick_t[...], tail_in[0]).astype(BF16)
+    out[...] = times(pick_t[...], home_in[...]) + times(behind, mix)
+    for copy in last_sends:
+        copy.wait_recv()
+    out[...] += times(times(pick_t[...], tail_in[1]).astype(BF16), own_low)
     stores.append(store(out, out_hbm.at[0]))
     for copy in sent:
         copy.wait_send()
@@ -209,11 +225,12 @@
     _, rank, features = adapter_down.shape
     columns = width // n_m
     tiles = features // min(512, features)
-    messages = TICKS + (n_q - 1) * (1 + TICKS) + 3 * (n_m - 1) + 2 * n_q + 2
+    pieces = 2 if features // n_q % 256 == 0 else 1
+    messages = TICKS * pieces * n_q + (n_q - 1) + (2 + TICKS) * (n_m - 1) + (1 + TICKS) * n_q + 2
     flops = 2 * slots * features * (2 * width + 3 * rank)
     vmem = pltpu.VMEM
     return pl.pallas_call(
-        functools.partial(kernel, counts),
+        functools.partial(kernel, counts, pieces),
         out_shape=(
             jax.ShapeDtypeStruct((1, slots, features), BF16),
             jax.ShapeDtypeStruct((1, slots, columns), F32),
@@ -235,17 +252,16 @@
             vmem((n_m - 1, slots + rank, columns), F32),
             vmem((slots, rank), F32),
             vmem((n_m - 1, slots, rank), F32),
-            vmem((slots + rank, TICKS * rank), F32),
-            vmem((n_m - 1, slots + rank, TICKS * rank), F32),
+            vmem((TICKS, slots + rank, rank), F32),
+            vmem((TICKS, n_m - 1, slots + rank, rank), F32),
             vmem((slots, columns), BF16),
             vmem((slots, columns), BF16),
-            vmem((slots, TICKS * rank), BF16),
-            vmem((slots, TICKS * rank), BF16),
+            vmem((TICKS, slots, rank), BF16),
+            vmem((TICKS, slots, rank), BF16),
             vmem((rank, columns), F32),
             vmem((rank, columns), F32),
-            vmem((rank, TICKS * rank), F32),
-            vmem((rank, TICKS * rank), F32),
-            vmem((TICKS * rank, columns), BF16),
+            vmem((rank, rank), F32),
+            vmem((rank, rank), F32),
             vmem((slots, columns), F32),
             pltpu.SemaphoreType.DMA((6 + n_m,)),
             pltpu.SemaphoreType.DMA((tiles + 1,)),
@@ -253,7 +269,7 @@
             pltpu.SemaphoreType.DMA((messages,)),
         ],
         compiler_params=pltpu.CompilerParams(
-            collective_id=0, has_side_effects=True, vmem_limit_bytes=48 * 1024 * 1024
+            collective_id=0, has_side_effects=True, vmem_limit_bytes=63 * 1024 * 1024
         ),
         cost_estimate=pl.CostEstimate(flops=flops, bytes_accessed=12 * 1024 * 1024, transcendentals=0),
     )(enc_rows, proj_weight, row_owner, grad_in, adapter_gain, adapter_down, adapter_up)

time: 43.5 us -> 39.4 us (0.906)
  the two profiles are of different devices: /device:TPU:9 before, /device:TPU:0 now
where the time goes in v2:
time: 39.4 us; the launch traced here: 39.2 us
  Pallas kernels  34.7 us (88%)
  local copies, waits for them, and re-layouts  3.88 us (10%)
  between operations  0.65 us (2%)
    pallas_call x1, Pallas kernels, on_device(): pl.pallas_call(functools.partial(kernel, counts, pieces), out_shape=(jax....  34.7 us
    unnamed x4, local copies, waits for them, and re-layouts  3.88 us

profile of v2, /device:TPU:0, one launch (start us, length us, event | category | flops | bytes accessed | tf_op | source)
XLA Modules:
  0.0 39.2 jit_solution(17749515214649657295)
XLA Ops:
  0.6 34.7 %shard_map.86 = (bf16[1,256,4096]{2,1,0:T(8,128)(2,1)}, f32[1,256,256]{2,1,0:T(8,128)}) custom-call(bf16[1,256,512]{2,1,0:T(8,128)(2,1)} %enc_hbm.1, bf16[512,4096]{1,0:T(8,128)(2,1)} %proj_hbm.1, s32[1,256]{1,0:T(1,128)} %owner_hbm.1, bf16[1,256,4096]{2,1,0:T(8,128)(2,1)} %grad_hbm.1, f32[1,4096]{1,0:T(1,128)} %gain_hbm.1, bf16[1,64,4096]{2,1,0:T(8,128)(2,1)} %down_hbm.1, ...), custom_call_target="tpu_custom_call" | custom-call | flops 2550136832 | bytes 12582912 | tf_op jit(solution)/shard_map/pallas_call | solution.py:232
  35.3 0.0 copy-start
  35.4 3.2 %copy.11 = bf16[1,256,4096]{2,1,0:T(8,128)(2,1)} copy(bf16[1,256,4096]{2,1,0:T(8,128)(2,1)} %get-tuple-element.4) | data formatting | bytes 4194304
  38.5 0.0 copy-done
  38.5 0.7 %copy.12 = f32[1,256,256]{2,1,0:T(8,128)} copy(f32[1,256,256]{2,1,0:T(8,128)S(1)} %copy-done) | data formatting | bytes 524288
Async XLA Ops:
  35.3 3.2 %copy-start = (f32[1,256,256]{2,1,0:T(8,128)S(1)}, f32[1,256,256]{2,1,0:T(8,128)}, u32[]{:S(2)}) copy-start(f32[1,256,256]{2,1,0:T(8,128)} %get-tuple-element.5) | copy-start | bytes 786436

commit v3 on v2

--- a/solution.py
+++ b/solution.py
@@ -27,8 +27,8 @@
 def kernel(
     counts, pieces,
     enc_hbm, proj_hbm, owner_hbm, grad_hbm, gain_hbm, down_hbm, up_hbm,
-    soft_hbm, out_hbm,
-    enc, owner, gain, down, x, w, staged, routed, pick_t, soft,
+    routed_hbm, out_hbm,
+    enc, owner, gain, down, x, w, staged, routed, pick_t,
     part, part_in, low, low_in, late, late_in,
     home, home_in, tail, tail_in, q_own, q_in, m_own, m_in, out,
     load_sem, store_sem, send_sem, recv_sem,
@@ -142,15 +142,18 @@
     down_load.wait()
     gain_load.wait()
     x[pl.ds(slots, rank), :] = (gain[...] * down[...].astype(F32)).astype(BF16)
-    pass_on(0, 0)
+    for h in range(pieces):
+        pass_on(0, h)
+    split = (n_m + 1) // 2
     for j in range(n_m):
+        if j == split:
+            for h in range(pieces):
+                pass_on(1, h)
         proj_loads[j].wait()
         part[j] = times_t(x[...], w[pl.ds(j * columns, columns), :])
     part_sends = [
         send(part.at[lax.rem(m + dm, n_m)], part_in.at[dm - 1], (0, 0, dm)) for dm in range(1, n_m)
     ]
-    for h in range(1, pieces):
-        pass_on(0, h)
     pick_t[...] = jnp.transpose(pick).astype(BF16)
 
     for copy in low_sends + part_sends:
@@ -163,9 +166,6 @@
     u_own = u_own.astype(BF16)
     q_own[...] = sums[slots:]
     home[...] = (sums[:slots] + times(u_own, sums[slots:].astype(BF16))).astype(BF16)
-    for tick in range(1, TICKS):
-        for h in range(pieces):
-            pass_on(tick, h)
     home_sends = [
         send(home.at[rows_of(dq)], home_in.at[own_rows], (dq, -TICKS, 0)) for dq in range(n_q)
     ]
@@ -173,17 +173,21 @@
 
     for copy in enc_sends:
         copy.wait_recv()
-    stores = []
-    tile = min(512, features)
-    for start in range(0, features, tile):
-        at = pl.ds(start, tile)
-        soft[:, at] = times(routed[...], w[pl.ds(0, width), at]).astype(BF16)
-        stores.append(store(soft.at[:, at], soft_hbm.at[0, :, at]))
+    stores = [store(routed, routed_hbm)]
+
+    def share_of(dq):
+        return pl.ds(aligned(lax.rem(q + dq, n_q) * share, share), share)
 
     def layer_products(tick):
-        for copy in spread[tick]:
-            copy.wait_recv()
-        late[tick] = times_t(x[...], w[up_rows[tick + 1], :])
+        rows = up_rows[tick + 1]
+        at = share_of(0)
+        total = times_t(x[:, at], w[rows, at])
+        for dq in range(1, n_q):
+            for h in range(pieces):
+                spread[tick][h * (n_q - 1) + dq - 1].wait_recv()
+            at = share_of(n_q - dq)
+            total += times_t(x[:, at], w[rows, at])
+        late[tick] = total
         late_sends = [send(late.at[tick], late_in.at[tick, dm - 1], (0, 0, dm)) for dm in range(1, n_m)]
         for copy in late_sends:
             copy.wait_recv()
@@ -224,15 +228,14 @@
     _, slots, width = enc_rows.shape
     _, rank, features = adapter_down.shape
     columns = width // n_m
-    tiles = features // min(512, features)
     pieces = 2 if features // n_q % 256 == 0 else 1
     messages = TICKS * pieces * n_q + (n_q - 1) + (2 + TICKS) * (n_m - 1) + (1 + TICKS) * n_q + 2
-    flops = 2 * slots * features * (2 * width + 3 * rank)
+    flops = 2 * slots * features * (width + 3 * rank)
     vmem = pltpu.VMEM
-    return pl.pallas_call(
+    routed, enc_grad = pl.pallas_call(
         functools.partial(kernel, counts, pieces),
         out_shape=(
-            jax.ShapeDtypeStruct((1, slots, features), BF16),
+            jax.ShapeDtypeStruct((slots, width), BF16),
             jax.ShapeDtypeStruct((1, slots, columns), F32),
         ),
         in_specs=[pl.BlockSpec(memory_space=pl.ANY)] * 7,
@@ -247,7 +250,6 @@
             vmem((slots, width), BF16),
             vmem((slots, width), BF16),
             vmem((slots, slots), BF16),
-            vmem((slots, features), BF16),
             vmem((n_m, slots + rank, columns), F32),
             vmem((n_m - 1, slots + rank, columns), F32),
             vmem((slots, rank), F32),
@@ -264,7 +266,7 @@
             vmem((rank, rank), F32),
             vmem((slots, columns), F32),
             pltpu.SemaphoreType.DMA((6 + n_m,)),
-            pltpu.SemaphoreType.DMA((tiles + 1,)),
+            pltpu.SemaphoreType.DMA((2,)),
             pltpu.SemaphoreType.DMA((messages,)),
             pltpu.SemaphoreType.DMA((messages,)),
         ],
@@ -273,6 +275,7 @@
         ),
         cost_estimate=pl.CostEstimate(flops=flops, bytes_accessed=12 * 1024 * 1024, transcendentals=0),
     )(enc_rows, proj_weight, row_owner, grad_in, adapter_gain, adapter_down, adapter_up)
+    return times(routed, proj_weight).astype(BF16)[None], enc_grad
 
 
 def solution(mesh):

time: 39.4 us -> 39.9 us (1.013)
  matrix products: 0 us -> 4.89 us
  local copies, waits for them, and re-layouts: 3.88 us -> 0.71 us
  Pallas kernels: 34.7 us -> 33.5 us
    dot_general x0 -> x1, matrix products: none -> 4.89 us  [times(): return jnp.dot(a, b, preferred_element_type=F32)]
    unnamed x4 -> x3, local copies, waits for them, and re-layouts: 3.88 us -> 0.71 us
    pallas_call x1, Pallas kernels: 34.7 us -> 33.5 us  [on_device(): pl.pallas_call(functools.partial(kernel, counts, pieces), out_shape=(jax....]
where the time goes in v3:
time: 39.9 us; the launch traced here: 39.8 us
  Pallas kernels  33.5 us (84%)
  matrix products  4.89 us (12%)
  local copies, waits for them, and re-layouts  0.71 us (2%)
  between operations  0.65 us (2%)
    pallas_call x1, Pallas kernels, on_device(): pl.pallas_call(functools.partial(kernel, counts, pieces), out_shape=(jax....  33.5 us
    dot_general x1, matrix products, times(): return jnp.dot(a, b, preferred_element_type=F32)  4.89 us

profile of v3, /device:TPU:0, one launch (start us, length us, event | category | flops | bytes accessed | tf_op | source)
XLA Modules:
  0.0 39.8 jit_solution(10922428702990481015)
XLA Ops:
  0.6 33.5 %shard_map.86 = (bf16[256,512]{1,0:T(8,128)(2,1)}, f32[1,256,256]{2,1,0:T(8,128)}) custom-call(bf16[1,256,512]{2,1,0:T(8,128)(2,1)} %enc_hbm.1, bf16[512,4096]{1,0:T(8,128)(2,1)} %proj_hbm.1, s32[1,256]{1,0:T(1,128)} %owner_hbm.1, bf16[1,256,4096]{2,1,0:T(8,128)(2,1)} %grad_hbm.1, f32[1,4096]{1,0:T(1,128)} %gain_hbm.1, bf16[1,64,4096]{2,1,0:T(8,128)(2,1)} %down_hbm.1, ...), custom_call_target="tpu_custom_call" | custom-call | flops 1476395008 | bytes 12582912 | tf_op jit(solution)/shard_map/pallas_call | solution.py:235
  34.2 0.0 copy-start
  34.2 4.9 %fusion = bf16[1,256,4096]{2,1,0:T(8,128)(2,1)} fusion(bf16[256,512]{1,0:T(8,128)(2,1)} %get-tuple-element.4, bf16[512,4096]{1,0:T(8,128)(2,1)} %proj_hbm.1), kind=kOutput, calls=%fused_computation.1 | convolution fusion | flops 1074790400 | bytes 6553600 | tf_op jit(solution)/shard_map/dot_general | solution.py:16
  39.1 0.0 copy-done
  39.1 0.7 %copy.10 = f32[1,256,256]{2,1,0:T(8,128)} copy(f32[1,256,256]{2,1,0:T(8,128)S(1)} %copy-done) | data formatting | bytes 524288
Async XLA Ops:
  34.2 4.9 %copy-start = (f32[1,256,256]{2,1,0:T(8,128)S(1)}, f32[1,256,256]{2,1,0:T(8,128)}, u32[]{:S(2)}) copy-start(f32[1,256,256]{2,1,0:T(8,128)} %get-tuple-element.9) | copy-start | bytes 786436

commit v4 on v3

--- a/solution.py
+++ b/solution.py
@@ -27,8 +27,8 @@
 def kernel(
     counts, pieces,
     enc_hbm, proj_hbm, owner_hbm, grad_hbm, gain_hbm, down_hbm, up_hbm,
-    routed_hbm, out_hbm,
-    enc, owner, gain, down, x, w, staged, routed, pick_t,
+    soft_hbm, out_hbm,
+    enc, owner, gain, down, x, w, staged, routed, pick_t, soft,
     part, part_in, low, low_in, late, late_in,
     home, home_in, tail, tail_in, q_own, q_in, m_own, m_in, out,
     load_sem, store_sem, send_sem, recv_sem,
@@ -88,6 +88,29 @@
     barrier = pltpu.get_barrier_semaphore()
     for dq, dz, dm in sorted(targets):
         pl.semaphore_signal(barrier, inc=1, device_id=device(-dq, -dz, -dm), device_id_type=MESH)
+
+    pl.semaphore_wait(barrier, len(targets))
+
+    piece = share // pieces
+    up_rows = [pl.ds(width + tick * rank, rank) for tick in range(TICKS + 1)]
+
+    def piece_at(h):
+        return pl.ds(aligned(q * share + h * piece, 128), piece)
+
+    ring = [
+        [
+            send(up_hbm.at[0, :, piece_at(h)], w.at[up_rows[1], piece_at(h)], (0, 1, 0))
+            for h in range(pieces)
+        ]
+    ] + [[] for _ in range(1, TICKS)]
+    spread = [[] for _ in range(TICKS)]
+
+    def pass_on(tick, h):
+        ring[tick][h].wait_recv()
+        here = w.at[up_rows[tick + 1], piece_at(h)]
+        if tick + 1 < TICKS:
+            ring[tick + 1].append(send(here, w.at[up_rows[tick + 2], piece_at(h)], (0, 1, 0)))
+        spread[tick] += [send(here, here, (dq, 0, 0)) for dq in range(1, n_q)]
 
     owner_load.wait()
     owners = owner[...].astype(F32)
@@ -102,29 +125,6 @@
     pick = jnp.where(row_at.astype(F32) == target, 1.0, 0.0)
     enc_load.wait()
     staged[...] = times(pick.astype(BF16), enc[...]).astype(BF16)
-    pl.semaphore_wait(barrier, len(targets))
-
-    piece = share // pieces
-    up_rows = [pl.ds(width + tick * rank, rank) for tick in range(TICKS + 1)]
-
-    def piece_at(h):
-        return pl.ds(aligned(q * share + h * piece, 128), piece)
-
-    ring = [
-        [
-            send(up_hbm.at[0, :, piece_at(h)], w.at[up_rows[1], piece_at(h)], (0, 1, 0))
-            for h in range(pieces)
-        ]
-    ] + [[] for _ in range(1, TICKS)]
-    spread = [[] for _ in range(TICKS)]
-
-    def pass_on(tick, h):
-        ring[tick][h].wait_recv()
-        here = w.at[up_rows[tick + 1], piece_at(h)]
-        if tick + 1 < TICKS:
-            ring[tick + 1].append(send(here, w.at[up_rows[tick + 2], piece_at(h)], (0, 1, 0)))
-        spread[tick] += [send(here, here, (dq, 0, 0)) for dq in range(1, n_q)]
-
     own_rows = pl.ds(aligned(q * per, per), per)
 
     def rows_of(dq):
@@ -134,6 +134,10 @@
         send(staged.at[rows_of(dq)], routed.at[own_rows], (dq, 0, 0)) for dq in range(1, n_q)
     ]
     routed[own_rows, :] = staged[own_rows, :]
+
+    for h in range(pieces):
+        pass_on(0, h)
+    pick_t[...] = jnp.transpose(pick).astype(BF16)
 
     grad_load.wait()
     low_load.wait()
@@ -142,43 +146,22 @@
     down_load.wait()
     gain_load.wait()
     x[pl.ds(slots, rank), :] = (gain[...] * down[...].astype(F32)).astype(BF16)
-    for h in range(pieces):
-        pass_on(0, h)
-    split = (n_m + 1) // 2
-    for j in range(n_m):
-        if j == split:
-            for h in range(pieces):
-                pass_on(1, h)
-        proj_loads[j].wait()
-        part[j] = times_t(x[...], w[pl.ds(j * columns, columns), :])
-    part_sends = [
-        send(part.at[lax.rem(m + dm, n_m)], part_in.at[dm - 1], (0, 0, dm)) for dm in range(1, n_m)
-    ]
-    pick_t[...] = jnp.transpose(pick).astype(BF16)
-
-    for copy in low_sends + part_sends:
-        copy.wait_recv()
-    u_own = low[...]
-    sums = part[m]
-    for dm in range(1, n_m):
-        u_own += low_in[dm - 1]
-        sums += part_in[dm - 1]
-    u_own = u_own.astype(BF16)
-    q_own[...] = sums[slots:]
-    home[...] = (sums[:slots] + times(u_own, sums[slots:].astype(BF16))).astype(BF16)
-    home_sends = [
-        send(home.at[rows_of(dq)], home_in.at[own_rows], (dq, -TICKS, 0)) for dq in range(n_q)
-    ]
-    q_send = send(q_own, q_in, (0, -1, 0))
-
-    for copy in enc_sends:
-        copy.wait_recv()
-    stores = [store(routed, routed_hbm)]
+    for tick in range(1, TICKS):
+        for h in range(pieces):
+            pass_on(tick, h)
+    for copy in proj_loads:
+        copy.wait()
+    part_sends = []
+    for dm in [*range(1, n_m), 0]:
+        block = pl.ds(aligned(lax.rem(m + dm, n_m) * columns, columns), columns)
+        part[dm] = times_t(x[...], w[block, :])
+        if dm:
+            part_sends.append(send(part.at[dm], part_in.at[dm - 1], (0, 0, dm)))
 
     def share_of(dq):
         return pl.ds(aligned(lax.rem(q + dq, n_q) * share, share), share)
 
-    def layer_products(tick):
+    def late_products(tick):
         rows = up_rows[tick + 1]
         at = share_of(0)
         total = times_t(x[:, at], w[rows, at])
@@ -188,7 +171,9 @@
             at = share_of(n_q - dq)
             total += times_t(x[:, at], w[rows, at])
         late[tick] = total
-        late_sends = [send(late.at[tick], late_in.at[tick, dm - 1], (0, 0, dm)) for dm in range(1, n_m)]
+        return [send(late.at[tick], late_in.at[tick, dm - 1], (0, 0, dm)) for dm in range(1, n_m)]
+
+    def late_rows(tick, late_sends):
         for copy in late_sends:
             copy.wait_recv()
         sums = late[tick]
@@ -201,10 +186,41 @@
         ]
         return tail_sends, sums[slots:]
 
-    tail_sends, low_mix = layer_products(0)
+    late_sends = late_products(0)
+    for copy in low_sends + part_sends:
+        copy.wait_recv()
+    u_own = low[...]
+    sums = part[0]
+    for dm in range(1, n_m):
+        u_own += low_in[dm - 1]
+        sums += part_in[dm - 1]
+    u_own = u_own.astype(BF16)
+    q_own[...] = sums[slots:]
+    q_send = send(q_own, q_in, (0, -1, 0))
+    home[...] = (sums[:slots] + times(u_own, sums[slots:].astype(BF16))).astype(BF16)
+    home_sends = [
+        send(home.at[rows_of(dq)], home_in.at[own_rows], (dq, -TICKS, 0)) for dq in range(n_q)
+    ]
+    tail_sends, low_mix = late_rows(0, late_sends)
     m_own[...] = low_mix
     m_send = send(m_own, m_in, (0, -1, 0))
-    last_sends, _ = layer_products(1)
+
+    for copy in enc_sends:
+        copy.wait_recv()
+    stores = []
+    tile = min(512, features)
+
+    def soft_tokens(tiles):
+        for t in tiles:
+            at = pl.ds(t * tile, tile)
+            soft[:, at] = times(routed[...], w[pl.ds(0, width), at]).astype(BF16)
+            stores.append(store(soft.at[:, at], soft_hbm.at[0, :, at]))
+
+    n_tiles = features // tile
+    late_sends = late_products(1)
+    soft_tokens(range(n_tiles // 4))
+    last_sends, _ = late_rows(1, late_sends)
+    soft_tokens(range(n_tiles // 4, n_tiles))
 
     for copy in home_sends + [q_send, m_send] + tail_sends:
         copy.wait_recv()
@@ -222,6 +238,20 @@
         copy.wait()
 
 
+def hand_on(soft_from, out_from, soft_to, out_to, sems):
+    slots = soft_from.shape[1]
+    bands = sems.shape[0] - 1
+    band = slots // bands
+    copies = [pltpu.make_async_copy(out_from, out_to, sems.at[bands])]
+    for i in range(bands):
+        at = pl.ds(i * band, band)
+        copies.append(pltpu.make_async_copy(soft_from.at[:, at], soft_to.at[:, at], sems.at[i]))
+    for copy in copies:
+        copy.start()
+    for copy in copies:
+        copy.wait()
+
+
 def on_device(enc_rows, proj_weight, row_owner, grad_in, adapter_gain, adapter_down, adapter_up):
     counts = tuple(lax.axis_size(axis) for axis in ("seq", "section", "mp"))
     n_q, n_z, n_m = counts
@@ -232,12 +262,13 @@
     messages = TICKS * pieces * n_q + (n_q - 1) + (2 + TICKS) * (n_m - 1) + (1 + TICKS) * n_q + 2
     flops = 2 * slots * features * (width + 3 * rank)
     vmem = pltpu.VMEM
-    routed, enc_grad = pl.pallas_call(
+    results = (
+        jax.ShapeDtypeStruct((1, slots, features), BF16),
+        jax.ShapeDtypeStruct((1, slots, columns), F32),
+    )
+    soft, enc_grad = pl.pallas_call(
         functools.partial(kernel, counts, pieces),
-        out_shape=(
-            jax.ShapeDtypeStruct((slots, width), BF16),
-            jax.ShapeDtypeStruct((1, slots, columns), F32),
-        ),
+        out_shape=results,
         in_specs=[pl.BlockSpec(memory_space=pl.ANY)] * 7,
         out_specs=(pl.BlockSpec(memory_space=pl.ANY),) * 2,
         scratch_shapes=[
@@ -250,6 +281,7 @@
             vmem((slots, width), BF16),
             vmem((slots, width), BF16),
             vmem((slots, slots), BF16),
+            vmem((slots, features), BF16),
             vmem((n_m, slots + rank, columns), F32),
             vmem((n_m - 1, slots + rank, columns), F32),
             vmem((slots, rank), F32),
@@ -266,7 +298,7 @@
             vmem((rank, rank), F32),
             vmem((slots, columns), F32),
             pltpu.SemaphoreType.DMA((6 + n_m,)),
-            pltpu.SemaphoreType.DMA((2,)),
+            pltpu.SemaphoreType.DMA((features // min(512, features) + 1,)),
             pltpu.SemaphoreType.DMA((messages,)),
             pltpu.SemaphoreType.DMA((messages,)),
         ],
@@ -275,7 +307,15 @@
         ),
         cost_estimate=pl.CostEstimate(flops=flops, bytes_accessed=12 * 1024 * 1024, transcendentals=0),
     )(enc_rows, proj_weight, row_owner, grad_in, adapter_gain, adapter_down, adapter_up)
-    return times(routed, proj_weight).astype(BF16)[None], enc_grad
+    return pl.pallas_call(
+        hand_on,
+        out_shape=results,
+        in_specs=[pl.BlockSpec(memory_space=pl.ANY)] * 2,
+        out_specs=(pl.BlockSpec(memory_space=pl.ANY),) * 2,
+        scratch_shapes=[pltpu.SemaphoreType.DMA((9,))],
+        compiler_params=pltpu.CompilerParams(vmem_limit_bytes=63 * 1024 * 1024),
+        cost_estimate=pl.CostEstimate(flops=0, bytes_accessed=5 * 1024 * 1024, transcendentals=0),
+    )(soft, enc_grad)
 
 
 def solution(mesh):

time: 39.9 us -> 109 us (2.73)
  Pallas kernels: 33.5 us -> 108 us
  matrix products: 4.89 us -> 0 us
    pallas_call x1 -> x2, Pallas kernels: 33.5 us -> 108 us  [the longest x1 72.7 us: on_device(): pl.pallas_call(hand_on, out_shape=results, in_specs=[pl.BlockSpec(memory_...]
    dot_general x1 -> x0, matrix products: 4.89 us -> none  [times(): return jnp.dot(a, b, preferred_element_type=F32)]
where the time goes in v4:
time: 109 us
  Pallas kernels  108 us (99%)
    pallas_call x1, Pallas kernels, on_device(): pl.pallas_call(hand_on, out_shape=results, in_specs=[pl.BlockSpec(memory_...  72.7 us
    pallas_call x1, Pallas kernels, on_device(): pl.pallas_call(functools.partial(kernel, counts, pieces), out_shape=resul...  35.6 us

profile of v4, /device:TPU:0, one launch (start us, length us, event | category | flops | bytes accessed | tf_op | source)
XLA Modules:
  0.0 108.9 jit_solution(15715347433655567650)
XLA Ops:
  0.6 35.6 %shard_map.86 = (bf16[1,256,4096]{2,1,0:T(8,128)(2,1)}, f32[1,256,256]{2,1,0:T(8,128)}) custom-call(bf16[1,256,512]{2,1,0:T(8,128)(2,1)} %enc_hbm.1, bf16[512,4096]{1,0:T(8,128)(2,1)} %proj_hbm.1, s32[1,256]{1,0:T(1,128)} %owner_hbm.1, bf16[1,256,4096]{2,1,0:T(8,128)(2,1)} %grad_hbm.1, f32[1,4096]{1,0:T(1,128)} %gain_hbm.1, bf16[1,64,4096]{2,1,0:T(8,128)(2,1)} %down_hbm.1, ...), custom_call_target="tpu_custom_call" | custom-call | flops 1476395008 | bytes 12582912 | tf_op jit(solution)/shard_map/pallas_call | solution.py:269
  36.3 72.7 %shard_map.87 = (bf16[1,256,4096]{2,1,0:T(8,128)(2,1)}, f32[1,256,256]{2,1,0:T(8,128)}) custom-call(bf16[1,256,4096]{2,1,0:T(8,128)(2,1)} %get-tuple-element.4.soft_from, f32[1,256,256]{2,1,0:T(8,128)} %get-tuple-element.5.out_from), custom_call_target="tpu_custom_call" | custom-call | bytes 5242880 | tf_op jit(solution)/shard_map/pallas_call | solution.py:310

commit v5 on v4

--- a/solution.py
+++ b/solution.py
@@ -82,7 +82,7 @@
     ]
 
     targets = {(dq, 0, 0) for dq in range(1, n_q)}
-    targets |= {(0, 1, 0), (0, -1 % n_z, 0)}
+    targets |= {(0, dz % n_z, 0) for dz in [-1, *range(1, TICKS + 1)]}
     targets |= {(dq, -TICKS % n_z, 0) for dq in range(n_q)}
     targets |= {(0, 0, dm) for dm in range(1, n_m)}
     barrier = pltpu.get_barrier_semaphore()
@@ -97,19 +97,19 @@
     def piece_at(h):
         return pl.ds(aligned(q * share + h * piece, 128), piece)
 
+    low_load.wait()
     ring = [
         [
-            send(up_hbm.at[0, :, piece_at(h)], w.at[up_rows[1], piece_at(h)], (0, 1, 0))
+            send(w.at[up_rows[0], piece_at(h)], w.at[up_rows[tick], piece_at(h)], (0, tick, 0))
             for h in range(pieces)
         ]
-    ] + [[] for _ in range(1, TICKS)]
+        for tick in range(1, TICKS + 1)
+    ]
     spread = [[] for _ in range(TICKS)]
 
     def pass_on(tick, h):
         ring[tick][h].wait_recv()
         here = w.at[up_rows[tick + 1], piece_at(h)]
-        if tick + 1 < TICKS:
-            ring[tick + 1].append(send(here, w.at[up_rows[tick + 2], piece_at(h)], (0, 1, 0)))
         spread[tick] += [send(here, here, (dq, 0, 0)) for dq in range(1, n_q)]
 
     owner_load.wait()
@@ -140,7 +140,6 @@
     pick_t[...] = jnp.transpose(pick).astype(BF16)
 
     grad_load.wait()
-    low_load.wait()
     low[...] = times_t(x[pl.ds(0, slots), :], w[up_rows[0], :])
     low_sends = [send(low, low_in.at[dm - 1], (0, 0, dm)) for dm in range(1, n_m)]
     down_load.wait()
@@ -238,17 +237,22 @@
         copy.wait()
 
 
-def hand_on(soft_from, out_from, soft_to, out_to, sems):
-    slots = soft_from.shape[1]
-    bands = sems.shape[0] - 1
+def hand_on(soft_from, out_from, soft_to, out_to, soft, out, in_sem, out_sem):
+    slots = soft.shape[0]
+    bands = in_sem.shape[0] - 1
     band = slots // bands
-    copies = [pltpu.make_async_copy(out_from, out_to, sems.at[bands])]
-    for i in range(bands):
-        at = pl.ds(i * band, band)
-        copies.append(pltpu.make_async_copy(soft_from.at[:, at], soft_to.at[:, at], sems.at[i]))
-    for copy in copies:
+    moves = [
+        (soft_from.at[0, pl.ds(i * band, band)], soft.at[pl.ds(i * band, band)], soft_to.at[0, pl.ds(i * band, band)])
+        for i in range(bands)
+    ] + [(out_from.at[0], out, out_to.at[0])]
+    loads = [pltpu.make_async_copy(a, b, in_sem.at[i]) for i, (a, b, _) in enumerate(moves)]
+    stores = [pltpu.make_async_copy(b, c, out_sem.at[i]) for i, (_, b, c) in enumerate(moves)]
+    for copy in loads:
         copy.start()
-    for copy in copies:
+    for before, after in zip(loads, stores):
+        before.wait()
+        after.start()
+    for copy in stores:
         copy.wait()
 
 
@@ -312,7 +316,12 @@
         out_shape=results,
         in_specs=[pl.BlockSpec(memory_space=pl.ANY)] * 2,
         out_specs=(pl.BlockSpec(memory_space=pl.ANY),) * 2,
-        scratch_shapes=[pltpu.SemaphoreType.DMA((9,))],
+        scratch_shapes=[
+            vmem((slots, features), BF16),
+            vmem((slots, columns), F32),
+            pltpu.SemaphoreType.DMA((9,)),
+            pltpu.SemaphoreType.DMA((9,)),
+        ],
         compiler_params=pltpu.CompilerParams(vmem_limit_bytes=63 * 1024 * 1024),
         cost_estimate=pl.CostEstimate(flops=0, bytes_accessed=5 * 1024 * 1024, transcendentals=0),
     )(soft, enc_grad)

time: 109 us -> 40.3 us (0.37)
  Pallas kernels: 108 us -> 39.5 us
    pallas_call x1, Pallas kernels: 72.7 us -> 2.5 us  [on_device(): pl.pallas_call(hand_on, out_shape=results, in_specs=[pl.BlockSpec(memory_...]
    pallas_call x1, Pallas kernels: 35.6 us -> 37 us  [on_device(): pl.pallas_call(functools.partial(kernel, counts, pieces), out_shape=resul...]
where the time goes in v5:
time: 40.3 us; the launch traced here: 40.2 us
  Pallas kernels  39.5 us (98%)
  between operations  0.64 us (2%)
    pallas_call x1, Pallas kernels, on_device(): pl.pallas_call(functools.partial(kernel, counts, pieces), out_shape=resul...  37 us
    pallas_call x1, Pallas kernels, on_device(): pl.pallas_call(hand_on, out_shape=results, in_specs=[pl.BlockSpec(memory_...  2.5 us

profile of v5, /device:TPU:0, one launch (start us, length us, event | category | flops | bytes accessed | tf_op | source)
XLA Modules:
  0.0 40.2 jit_solution(6601392767011319844)
XLA Ops:
  0.6 37.0 %shard_map.86 = (bf16[1,256,4096]{2,1,0:T(8,128)(2,1)}, f32[1,256,256]{2,1,0:T(8,128)}) custom-call(bf16[1,256,512]{2,1,0:T(8,128)(2,1)} %enc_hbm.1, bf16[512,4096]{1,0:T(8,128)(2,1)} %proj_hbm.1, s32[1,256]{1,0:T(1,128)} %owner_hbm.1, bf16[1,256,4096]{2,1,0:T(8,128)(2,1)} %grad_hbm.1, f32[1,4096]{1,0:T(1,128)} %gain_hbm.1, bf16[1,64,4096]{2,1,0:T(8,128)(2,1)} %down_hbm.1, ...), custom_call_target="tpu_custom_call" | custom-call | flops 1476395008 | bytes 12582912 | tf_op jit(solution)/shard_map/pallas_call | solution.py:273
  37.7 2.5 %shard_map.87 = (bf16[1,256,4096]{2,1,0:T(8,128)(2,1)}, f32[1,256,256]{2,1,0:T(8,128)}) custom-call(bf16[1,256,4096]{2,1,0:T(8,128)(2,1)} %get-tuple-element.4.soft_from, f32[1,256,256]{2,1,0:T(8,128)} %get-tuple-element.5.out_from), custom_call_target="tpu_custom_call" | custom-call | bytes 5242880 | tf_op jit(solution)/shard_map/pallas_call | solution.py:314

commit v6 on v5

--- a/solution.py
+++ b/solution.py
@@ -31,7 +31,7 @@
     enc, owner, gain, down, x, w, staged, routed, pick_t, soft,
     part, part_in, low, low_in, late, late_in,
     home, home_in, tail, tail_in, q_own, q_in, m_own, m_in, out,
-    load_sem, store_sem, send_sem, recv_sem,
+    load_sem, store_sem, send_sem, recv_sem, line_send, line_recv, spread_send, spread_recv,
 ):
     n_q, n_z, n_m = counts
     q, z, m = lax.axis_index("seq"), lax.axis_index("section"), lax.axis_index("mp")
@@ -82,7 +82,7 @@
     ]
 
     targets = {(dq, 0, 0) for dq in range(1, n_q)}
-    targets |= {(0, dz % n_z, 0) for dz in [-1, *range(1, TICKS + 1)]}
+    targets |= {(0, dz % n_z, 0) for dz in (-1, 1)}
     targets |= {(dq, -TICKS % n_z, 0) for dq in range(n_q)}
     targets |= {(0, 0, dm) for dm in range(1, n_m)}
     barrier = pltpu.get_barrier_semaphore()
@@ -97,20 +97,64 @@
     def piece_at(h):
         return pl.ds(aligned(q * share + h * piece, 128), piece)
 
+    if n_z == 4 and TICKS == 2:
+        plan = [(0, 1, 1, (0, 1, 2)), (0, 2, -2, (2, 3)), (1, 2, 1, (1, 2)), (2, 1, -1, (1,))]
+        swapped = z == 0
+    else:
+        plan = [(tick, tick + 1, 1, None) for tick in range(TICKS)]
+        swapped = None
+
+    def only(sections, act):
+        if sections is None:
+            act()
+        else:
+            chosen = z == sections[0]
+            for section in sections[1:]:
+                chosen = jnp.logical_or(chosen, z == section)
+            pl.when(chosen)(act)
+
+    def along(entry, h):
+        source, slot, dz, _ = plan[entry]
+        return pltpu.make_async_remote_copy(
+            src_ref=w.at[up_rows[source], piece_at(h)], dst_ref=w.at[up_rows[slot], piece_at(h)],
+            send_sem=line_send.at[entry * pieces + h], recv_sem=line_recv.at[(slot - 1) * pieces + h],
+            device_id=device(0, dz, 0), device_id_type=MESH,
+        )
+
+    def send_from(slot, h):
+        for entry, (source, _, _, sections) in enumerate(plan):
+            if source == slot:
+                only(sections, along(entry, h).start)
+
     low_load.wait()
-    ring = [
-        [
-            send(w.at[up_rows[0], piece_at(h)], w.at[up_rows[tick], piece_at(h)], (0, tick, 0))
-            for h in range(pieces)
-        ]
-        for tick in range(1, TICKS + 1)
+    for h in range(pieces):
+        send_from(0, h)
+
+    def described(tick, h, dq):
+        here = w.at[up_rows[tick + 1], piece_at(h)]
+        at = (tick * pieces + h) * (n_q - 1) + dq - 1
+        return pltpu.make_async_remote_copy(
+            src_ref=here, dst_ref=here, send_sem=spread_send.at[at], recv_sem=spread_recv.at[at],
+            device_id=device(dq, 0, 0), device_id_type=MESH,
+        )
+
+    spread = [
+        [described(tick, h, dq) for h in range(pieces) for dq in range(1, n_q)] for tick in range(TICKS)
     ]
-    spread = [[] for _ in range(TICKS)]
-
-    def pass_on(tick, h):
-        ring[tick][h].wait_recv()
-        here = w.at[up_rows[tick + 1], piece_at(h)]
-        spread[tick] += [send(here, here, (dq, 0, 0)) for dq in range(1, n_q)]
+
+    def pass_slot(tick):
+        for h in range(pieces):
+            along([slot for _, slot, _, _ in plan].index(tick + 1), h).wait_recv()
+            send_from(tick + 1, h)
+            for dq in range(1, n_q):
+                spread[tick][h * (n_q - 1) + dq - 1].start()
+
+    def pass_on(tick):
+        if swapped is None:
+            pass_slot(tick)
+        else:
+            pl.when(swapped)(lambda: pass_slot(TICKS - 1 - tick))
+            pl.when(jnp.logical_not(swapped))(lambda: pass_slot(tick))
 
     owner_load.wait()
     owners = owner[...].astype(F32)
@@ -135,8 +179,7 @@
     ]
     routed[own_rows, :] = staged[own_rows, :]
 
-    for h in range(pieces):
-        pass_on(0, h)
+    pass_on(0)
     pick_t[...] = jnp.transpose(pick).astype(BF16)
 
     grad_load.wait()
@@ -146,8 +189,7 @@
     gain_load.wait()
     x[pl.ds(slots, rank), :] = (gain[...] * down[...].astype(F32)).astype(BF16)
     for tick in range(1, TICKS):
-        for h in range(pieces):
-            pass_on(tick, h)
+        pass_on(tick)
     for copy in proj_loads:
         copy.wait()
     part_sends = []
@@ -231,8 +273,11 @@
         copy.wait_recv()
     out[...] += times(times(pick_t[...], tail_in[1]).astype(BF16), own_low)
     stores.append(store(out, out_hbm.at[0]))
-    for copy in sent:
+    for copy in sent + [copy for copies in spread for copy in copies]:
         copy.wait_send()
+    for entry, (_, _, _, sections) in enumerate(plan):
+        for h in range(pieces):
+            only(sections, along(entry, h).wait_send)
     for copy in stores:
         copy.wait()
 
@@ -263,7 +308,7 @@
     _, rank, features = adapter_down.shape
     columns = width // n_m
     pieces = 2 if features // n_q % 256 == 0 else 1
-    messages = TICKS * pieces * n_q + (n_q - 1) + (2 + TICKS) * (n_m - 1) + (1 + TICKS) * n_q + 2
+    messages = (n_q - 1) + (2 + TICKS) * (n_m - 1) + (1 + TICKS) * n_q + 2
     flops = 2 * slots * features * (width + 3 * rank)
     vmem = pltpu.VMEM
     results = (
@@ -305,6 +350,10 @@
             pltpu.SemaphoreType.DMA((features // min(512, features) + 1,)),
             pltpu.SemaphoreType.DMA((messages,)),
             pltpu.SemaphoreType.DMA((messages,)),
+            pltpu.SemaphoreType.DMA((2 * TICKS * pieces,)),
+            pltpu.SemaphoreType.DMA((TICKS * pieces,)),
+            pltpu.SemaphoreType.DMA((TICKS * pieces * (n_q - 1),)),
+            pltpu.SemaphoreType.DMA((TICKS * pieces * (n_q - 1),)),
         ],
         compiler_params=pltpu.CompilerParams(
             collective_id=0, has_side_effects=True, vmem_limit_bytes=63 * 1024 * 1024

time: 40.3 us -> 38.2 us (0.948)
  Pallas kernels: 39.5 us -> 37.4 us
    pallas_call x1, Pallas kernels: 37 us -> 34.9 us  [on_device(): pl.pallas_call(functools.partial(kernel, counts, pieces), out_shape=resul...]
where the time goes in v6:
time: 38.2 us; the launch traced here: 38.1 us
  Pallas kernels  37.4 us (98%)
  between operations  0.64 us (2%)
    pallas_call x1, Pallas kernels, on_device(): pl.pallas_call(functools.partial(kernel, counts, pieces), out_shape=resul...  34.9 us
    pallas_call x1, Pallas kernels, on_device(): pl.pallas_call(hand_on, out_shape=results, in_specs=[pl.BlockSpec(memory_...  2.5 us

profile of v6, /device:TPU:0, one launch (start us, length us, event | category | flops | bytes accessed | tf_op | source)
XLA Modules:
  0.0 38.1 jit_solution(14151058360613794640)
XLA Ops:
  0.6 34.9 %shard_map.86 = (bf16[1,256,4096]{2,1,0:T(8,128)(2,1)}, f32[1,256,256]{2,1,0:T(8,128)}) custom-call(bf16[1,256,512]{2,1,0:T(8,128)(2,1)} %enc_hbm.1, bf16[512,4096]{1,0:T(8,128)(2,1)} %proj_hbm.1, s32[1,256]{1,0:T(1,128)} %owner_hbm.1, bf16[1,256,4096]{2,1,0:T(8,128)(2,1)} %grad_hbm.1, f32[1,4096]{1,0:T(1,128)} %gain_hbm.1, bf16[1,64,4096]{2,1,0:T(8,128)(2,1)} %down_hbm.1, ...), custom_call_target="tpu_custom_call" | custom-call | flops 1476395008 | bytes 12582912 | tf_op jit(solution)/shard_map/pallas_call | solution.py:318
  35.6 2.5 %shard_map.87 = (bf16[1,256,4096]{2,1,0:T(8,128)(2,1)}, f32[1,256,256]{2,1,0:T(8,128)}) custom-call(bf16[1,256,4096]{2,1,0:T(8,128)(2,1)} %get-tuple-element.4.soft_from, f32[1,256,256]{2,1,0:T(8,128)} %get-tuple-element.5.out_from), custom_call_target="tpu_custom_call" | custom-call | bytes 5242880 | tf_op jit(solution)/shard_map/pallas_call | solution.py:363

commit v7 on v6

--- a/solution.py
+++ b/solution.py
@@ -258,10 +258,9 @@
             stores.append(store(soft.at[:, at], soft_hbm.at[0, :, at]))
 
     n_tiles = features // tile
+    soft_tokens(range(n_tiles))
     late_sends = late_products(1)
-    soft_tokens(range(n_tiles // 4))
     last_sends, _ = late_rows(1, late_sends)
-    soft_tokens(range(n_tiles // 4, n_tiles))
 
     for copy in home_sends + [q_send, m_send] + tail_sends:
         copy.wait_recv()

time: 38.2 us -> 38.1 us (level)
  no operation moved by 1% of the time
where the time goes in v7:
time: 38.1 us; the launch traced here: 38 us
  Pallas kernels  37.3 us (98%)
  between operations  0.64 us (2%)
    pallas_call x1, Pallas kernels, on_device(): pl.pallas_call(functools.partial(kernel, counts, pieces), out_shape=resul...  34.8 us
    pallas_call x1, Pallas kernels, on_device(): pl.pallas_call(hand_on, out_shape=results, in_specs=[pl.BlockSpec(memory_...  2.5 us

profile of v7, /device:TPU:0, one launch (start us, length us, event | category | flops | bytes accessed | tf_op | source)
XLA Modules:
  0.0 38.0 jit_solution(17397257348507346755)
XLA Ops:
  0.6 34.8 %shard_map.86 = (bf16[1,256,4096]{2,1,0:T(8,128)(2,1)}, f32[1,256,256]{2,1,0:T(8,128)}) custom-call(bf16[1,256,512]{2,1,0:T(8,128)(2,1)} %enc_hbm.1, bf16[512,4096]{1,0:T(8,128)(2,1)} %proj_hbm.1, s32[1,256]{1,0:T(1,128)} %owner_hbm.1, bf16[1,256,4096]{2,1,0:T(8,128)(2,1)} %grad_hbm.1, f32[1,4096]{1,0:T(1,128)} %gain_hbm.1, bf16[1,64,4096]{2,1,0:T(8,128)(2,1)} %down_hbm.1, ...), custom_call_target="tpu_custom_call" | custom-call | flops 1476395008 | bytes 12582912 | tf_op jit(solution)/shard_map/pallas_call | solution.py:317
  35.5 2.5 %shard_map.87 = (bf16[1,256,4096]{2,1,0:T(8,128)(2,1)}, f32[1,256,256]{2,1,0:T(8,128)}) custom-call(bf16[1,256,4096]{2,1,0:T(8,128)(2,1)} %get-tuple-element.4.soft_from, f32[1,256,256]{2,1,0:T(8,128)} %get-tuple-element.5.out_from), custom_call_target="tpu_custom_call" | custom-call | bytes 5242880 | tf_op jit(solution)/shard_map/pallas_call | solution.py:362
